TPU v7x, 32 devices: a whole 2x2x4 slice. The times are simulated.
32 devices in a mesh: parts: 2 (over y), tensor: 4 (over z), dp: 4 (over x, core).
Axes of the slice: x: 2, y: 2, z: 4, core: 2. Of those that a mesh axis runs over, the one named last changes fastest.
Arguments:
- tokens: bfloat16 [1024, 8192], P(('parts', 'dp'), 'tensor'), parts along dimension 0, may hold values from -6 to 6
- weight: bfloat16 [8192, 8192], P(None, 'tensor'), may hold values from -0.0625 to 0.0625
- adapter_down_factor: bfloat16 [8, 8192, 256], P(('parts', 'dp'), 'tensor'), parts along dimension 0, may hold values from -0.0625 to 0.0625
- adapter_up_factor: bfloat16 [8, 256, 8192], P(('parts', 'dp'), None, 'tensor'), parts along dimension 0, may hold values from -0.375 to 0.375
- cotangent: bfloat16 [1024, 8192], P(('parts', 'dp'), 'tensor'), parts along dimension 0, may hold values from -6 to 6
- micro_destination_group: int32 [64, 1], P('parts'), parts along dimension 0, may hold values from 0 to 3; in each aligned block of 8 rows (0 to 7, 8 to 15, ...) at most 2 rows name the same one
- micro_adapter: int32 [64], P('parts'), parts along dimension 0, may hold values from 0 to 3
- micro_token_count: int32 [64], P('parts'), parts along dimension 0, may hold values from 12 to 16
- adapter_rank_bucket: int32 [8], P('parts'), parts along dimension 0, may hold values from 0 to 2, as said below
- adapter_home_row: int32 [8], P('parts'), parts along dimension 0, may hold values from 0 to 3, each once
Outputs:
- outputs: bfloat16 [1024, 8192], P(('parts', 'dp'), 'tensor'), parts along dimension 0
- packed_input_gradient: bfloat16 [1024, 8192], P(('parts', 'dp'), 'tensor'), parts along dimension 0
- grad_a: bfloat16 [8, 8192, 256], P(('parts', 'dp'), 'tensor'), parts along dimension 0
- grad_b: bfloat16 [8, 256, 8192], P(('parts', 'dp'), None, 'tensor'), parts along dimension 0
There are 2 independent parts, one for each index of `parts`. A program takes and returns all parts, laid end to end along the dimension named above; an argument that names none is the same for every part. Nothing has to cross between parts.
Inputs may be any that keep to these rules, and one draw needn't show every extreme that they name: `micro_destination_group`: within the 8 micro-batches of one source group no destination group is named more than 2 times. `micro_token_count`: tokens 0 to count - 1 of a micro-batch are live. `adapter_rank_bucket`: an adapter's rank is 16 times 4 to the power of its bucket. `adapter_home_row`: A permutation.
All inputs are finite; a program needn't handle non-finite values.
Results may differ from a plain program's by a relative error of at most 0.015.
Values may be sent and summed in bfloat16 or wider, within the bound.
A program may use at most 192 MiB of HBM per device.

v0:
```python
import jax
import jax.numpy as jnp
from jax import lax
from jax.sharding import PartitionSpec as P

RANK_LOW = 16
LARGEST_RANK = 256
CAP = 2
MICRO_TOKENS = 16


def swap(value, bit, n):
    return lax.ppermute(value, "dp", [(i, i ^ bit) for i in range(n)])


def offsets_of(n):
    offsets = [0]
    bit = n // 2
    while bit:
        offsets += [o ^ bit for o in offsets]
        bit //= 2
    return offsets


def gather_blocks(value, n):
    blocks = {0: value}
    bit = n // 2
    while bit:
        for o in list(blocks):
            blocks[o ^ bit] = swap(blocks[o], bit, n)
        bit //= 2
    return jnp.concatenate([blocks[o] for o in offsets_of(n)], axis=0)


def reduce_blocks(value, n):
    rows = value.shape[0] // n
    blocks = {o: value[j * rows : (j + 1) * rows] for j, o in enumerate(offsets_of(n))}
    bit = 1
    while bit < n:
        blocks = {o: blocks[o] + swap(blocks[o | bit], bit, n) for o in blocks if not o & bit}
        bit *= 2
    return blocks[0]


def rows_of(values):
    return jnp.repeat(values, MICRO_TOKENS)


def packing(micro_destination_group, micro_adapter, micro_token_count, adapter_home_row, n, me):
    groups = micro_destination_group[:, 0]
    count_all = groups.shape[0]
    per_group = count_all // n
    indices = jnp.arange(count_all, dtype=jnp.int32)
    source = indices // per_group
    earlier = (
        (groups[:, None] == groups[None, :])
        & (source[:, None] == source[None, :])
        & (indices[None, :] < indices[:, None])
    )
    placing = jnp.sum(earlier.astype(jnp.int32), axis=1)
    target = groups * (n * CAP) + source * CAP + placing
    peers = me ^ jnp.array(offsets_of(n), dtype=jnp.int32)
    micro_ids = (
        peers[:, None] * per_group + jnp.arange(per_group, dtype=jnp.int32)[None, :]
    ).reshape(-1)
    slot_ids = (peers[:, None] * (n * CAP) + jnp.arange(n * CAP, dtype=jnp.int32)[None, :]).reshape(
        -1
    )
    here = (micro_ids[:, None] == indices[None, :]).astype(jnp.int32)
    micro_target = jnp.sum(here * target[None, :], axis=1)
    select = (slot_ids[:, None] == target[None, :]).astype(jnp.int32)
    adapter = jnp.sum(select * micro_adapter[None, :], axis=1)
    counted = jnp.sum(select * micro_token_count[None, :], axis=1)
    table_ids = jnp.arange(adapter_home_row.shape[0], dtype=jnp.int32)
    matches = (adapter[:, None] == table_ids[None, :]).astype(jnp.int32)
    home = jnp.sum(matches * adapter_home_row[None, :], axis=1)
    return micro_target, slot_ids, home, counted


def local(
    tokens,
    weight,
    adapter_down_factor,
    adapter_up_factor,
    cotangent,
    micro_destination_group,
    micro_adapter,
    micro_token_count,
    adapter_rank_bucket,
    adapter_home_row,
):
    n = lax.axis_size("dp")
    me = lax.axis_index("dp")
    n_tensor = lax.axis_size("tensor")
    features = tokens.shape[1]
    own_rows = cotangent.shape[0]
    f32, bf16 = jnp.float32, jnp.bfloat16
    down, up = adapter_down_factor[0], adapter_up_factor[0]

    x_all = gather_blocks(tokens, n)
    dy_all = gather_blocks(cotangent, n)

    back_part = lax.dot_general(
        weight, cotangent, (((1,), (1,)), ((), ())), preferred_element_type=f32
    ).astype(bf16)
    back = lax.psum_scatter(back_part, "tensor", scatter_dimension=0, tiled=True).T

    micro_target, slot_ids, home, counted = packing(
        micro_destination_group, micro_adapter, micro_token_count, adapter_home_row, n, me
    )
    token = jnp.arange(x_all.shape[0], dtype=jnp.int32) % MICRO_TOKENS
    place = jnp.arange(dy_all.shape[0], dtype=jnp.int32) % MICRO_TOKENS
    move = (
        (rows_of(slot_ids) * MICRO_TOKENS + place)[:, None]
        == (rows_of(micro_target) * MICRO_TOKENS + token)[None, :]
    ).astype(bf16)
    live = place < rows_of(counted)
    mine = (live & (rows_of(home) == me)).astype(f32)[:, None]
    own_live = live[:own_rows].astype(f32)[:, None]
    bucket = jnp.sum(jnp.where(adapter_home_row == me, adapter_rank_bucket, 0))
    rank = RANK_LOW * jnp.where(bucket == 0, 1, jnp.where(bucket == 1, 4, 16))
    scale = jnp.sqrt(LARGEST_RANK / rank.astype(f32))
    columns = (jnp.arange(LARGEST_RANK, dtype=jnp.int32) < rank).astype(f32)[None, :]

    x_own = jnp.dot(move[:own_rows], x_all, preferred_element_type=f32).astype(bf16)
    x_full = lax.all_gather(x_own, "tensor", axis=1, tiled=True)
    base = jnp.dot(x_full, weight, preferred_element_type=f32)

    u_part = jnp.dot(x_all, down, preferred_element_type=f32).astype(bf16)
    g_part = lax.dot_general(
        dy_all, up, (((1,), (1,)), ((), ())), preferred_element_type=f32
    ).astype(bf16)
    u_sum, g_sum = lax.psum(u_part, "tensor"), lax.psum(g_part, "tensor")

    low_source = (u_sum.astype(f32) * columns).astype(bf16)
    low = (jnp.dot(move, low_source, preferred_element_type=f32) * mine).astype(bf16)
    grad_low = (g_sum.astype(f32) * columns * scale * mine).astype(bf16)
    grad_low_source = lax.dot_general(
        move, grad_low, (((0,), (0,)), ((), ())), preferred_element_type=f32
    ).astype(bf16)

    out_delta = (scale * jnp.dot(low, up, preferred_element_type=f32)).astype(bf16)
    out_delta = reduce_blocks(out_delta, n)
    back_delta = lax.dot_general(
        grad_low, down, (((1,), (1,)), ((), ())), preferred_element_type=f32
    ).astype(bf16)
    back_delta = reduce_blocks(back_delta, n)

    grad_a = lax.dot_general(
        x_all, grad_low_source, (((0,), (0,)), ((), ())), preferred_element_type=f32
    )
    grad_b = scale * lax.dot_general(
        low, dy_all, (((0,), (0,)), ((), ())), preferred_element_type=f32
    )
    outputs = own_live * (base + out_delta.astype(f32))
    input_gradient = own_live * (back.astype(f32) + back_delta.astype(f32))
    return (
        outputs.astype(bf16),
        input_gradient.astype(bf16),
        grad_a.astype(bf16)[None],
        grad_b.astype(bf16)[None],
    )


def solution(mesh):
    in_specs = (
        P(("parts", "dp"), "tensor"),
        P(None, "tensor"),
        P(("parts", "dp"), "tensor", None),
        P(("parts", "dp"), None, "tensor"),
        P(("parts", "dp"), "tensor"),
        P("parts", None),
        P("parts"),
        P("parts"),
        P("parts"),
        P("parts"),
    )
    out_specs = (
        P(("parts", "dp"), "tensor"),
        P(("parts", "dp"), "tensor"),
        P(("parts", "dp"), "tensor", None),
        P(("parts", "dp"), None, "tensor"),
    )
    return jax.shard_map(local, mesh=mesh, in_specs=in_specs, out_specs=out_specs, check_vma=False)
```

profile of v0, /device:TPU:0, one launch (start us, length us, event | category | flops | bytes accessed | tf_op | source)
XLA Modules:
  0.0 188.1 jit_solution(6225462203596368187)
XLA Ops:
  7.2 3.0 %collective-permute-start = (bf16[128,2048]{1,0:T(8,128)(2,1)}, bf16[128,2048]{1,0:T(8,128)(2,1)}, u32[]{:S(2)}, u32[]{:S(2)}) collective-permute-start(bf16[128,2048]{1,0:T(8,128)(2,1)} %param.11), channel_id=1, source_target_pairs={{0,2},{1,3},{2,0},{3,1},{4,6},{5,7},{6,4},{7,5},{8,10},{9,11},{10,... | collective-permute-start | bytes 1572872 | tf_op jit(solution)/shard_map/ppermute | solution.py:13
  10.7 1.1 constant_dynamic-update-slice_fusion.3
  11.8 0.9 convert_reduce_fusion
  13.4 1.3 fusion.32
  15.9 1.9 %constant_dynamic-update-slice_fusion.7 = bf16[512,2048]{1,0:T(8,128)(2,1)} fusion(bf16[128,2048]{1,0:T(8,128)(2,1)} %param.15), kind=kLoop, calls=%fused_computation.48 | loop fusion | bytes 1048576
  18.0 5.3 %collective-permute-done = bf16[128,2048]{1,0:T(8,128)(2,1)} collective-permute-done((bf16[128,2048]{1,0:T(8,128)(2,1)}, bf16[128,2048]{1,0:T(8,128)(2,1)}, u32[]{:S(2)}, u32[]{:S(2)}) %collective-permute-start) | collective-permute-done | bytes 524320 | tf_op jit(solution)/shard_map/ppermute | solution.py:13
  23.3 10.4 %collective-permute-done.6 = bf16[128,2048]{1,0:T(8,128)(2,1)} collective-permute-done((bf16[128,2048]{1,0:T(8,128)(2,1)}, bf16[128,2048]{1,0:T(8,128)(2,1)}, u32[]{:S(2)}, u32[]{:S(2)}) %collective-permute-start.6) | collective-permute-done | bytes 524320 | tf_op jit(solution)/shard_map/ppermute | solution.py:13
  33.7 1.1 constant_dynamic-update-slice_fusion.2
  34.8 1.9 constant_dynamic-update-slice_fusion.6
  36.7 1.1 constant_dynamic-update-slice_fusion.1
  37.8 1.9 %constant_dynamic-update-slice_fusion.5 = bf16[512,2048]{1,0:T(8,128)(2,1)} fusion(bf16[512,2048]{1,0:T(8,128)(2,1)} %constant_dynamic-update-slice_fusion.6, bf16[128,2048]{1,0:T(8,128)(2,1)} %collective-permute-done.7), kind=kLoop, calls=%fused_computation.46 | loop fusion | bytes 1048576
  39.8 1.4 convolution_convert_fusion.6
  41.2 1.0 copy-done.3
  42.2 1.4 copy-done.4
  43.6 1.5 convolution_convert_fusion.5
  45.4 1.2 convolution_convert_fusion.3
  46.9 23.2 %convolution_convert_fusion = bf16[8192,128]{0,1:T(8,128)(2,1)} fusion(bf16[8192,2048]{1,0:T(8,128)(2,1)} %param.12, bf16[128,2048]{1,0:T(8,128)(2,1)} %param.15), kind=kOutput, calls=%fused_computation | convolution fusion | flops 4296015872 | bytes 36175872 | tf_op jit(solution)/shard_map/dot_general | solution.py:103
  71.9 13.4 %all-reduce.3.cloned.1.call-done = (bf16[512,256]{1,0:T(8,128)(2,1)}, bf16[512,256]{1,0:T(8,128)(2,1)}) async-done(((bf16[512,256]{1,0:T(8,128)(2,1)}, bf16[512,256]{1,0:T(8,128)(2,1)}), (bf16[512,256]{1,0:T(8,128)(2,1)}, bf16[512,256]{1,0:T(8,128)(2,1)})) %all-reduce.3.cloned.1.call-update) | async-done | bytes 524304 | tf_op jit(solution)/shard_map/psum | solution.py:133
  85.4 1.3 fusion.3
  86.7 1.8 convolution_convert_fusion.1
  88.5 1.0 fusion.34
  90.3 1.3 copy-done.1
  91.6 1.1 fusion.35
  93.2 4.1 %fusion.1 = bf16[1,2048,256]{2,1,0:T(8,128)(2,1)} fusion(bf16[512,2048]{1,0:T(8,128)(2,1)} %copy-done.2, s32[512]{0:T(512)S(1)} %fusion.28, s32[512]{0:T(512)S(1)} %fusion.29, bf16[512,256]{1,0:T(8,128)(2,1)} %get-tuple-element.8, f32[]{:T(128)S(6)} %sqrt.3, f32[512]{0:T(512)S(1)} %get-tuple-element.9, f32[256]{0:T(256)S(1)} %compare_convert_fusion), kind=kOutput, calls=%fused_computation.6 | convolution fusion | flops 672661504 | bytes 3415044 | tf_op jit(solution)/shard_map/dot_general | solution.py:149
  97.3 3.3 %fusion.2 = bf16[1,256,2048]{2,1,0:T(8,128)(2,1)} fusion(bf16[512,256]{1,0:T(8,128)(2,1)S(1)} %fusion.3, bf16[512,2048]{1,0:T(8,128)(2,1)} %copy-done.4, f32[]{:T(128)S(6)} %sqrt.3), kind=kOutput, calls=%fused_computation.7 | convolution fusion | flops 537919488 | bytes 3407876 | tf_op jit(solution)/shard_map/dot_general | solution.py:152
  101.1 1.9 %slice_add_fusion = bf16[128,2048]{1,0:T(8,128)(2,1)} fusion(bf16[128,2048]{1,0:T(8,128)(2,1)} %collective-permute-done.10, bf16[512,2048]{1,0:T(8,128)(2,1)S(1)} %convolution_convert_fusion.1), kind=kLoop, calls=%fused_computation.24 | loop fusion | flops 262144 | bytes 1572864 | tf_op jit(solution)/shard_map/add | solution.py:40
  103.0 1.5 collective-permute-start.11
  104.5 2.1 %slice_add_fusion.2 = bf16[128,2048]{1,0:T(8,128)(2,1)} fusion(bf16[128,2048]{1,0:T(8,128)(2,1)} %collective-permute-done.4, bf16[512,2048]{1,0:T(8,128)(2,1)} %copy-done.1), kind=kLoop, calls=%fused_computation.27 | loop fusion | flops 262144 | bytes 1572864 | tf_op jit(solution)/shard_map/add | solution.py:40
  107.1 25.8 %all-gather.2.cloned.1.call-done = bf16[128,8192]{1,0:T(8,128)(2,1)} async-done(((bf16[128,2048]{1,0:T(8,128)(2,1)}), bf16[128,8192]{1,0:T(8,128)(2,1)}) %all-gather.2.cloned.1.call-update) | async-done | bytes 2097168 | tf_op jit(solution)/shard_map/all_gather | solution.py:126
  132.9 17.3 %fusion.36 = f32[128,2048]{1,0:T(8,128)} fusion(bf16[128,8192]{1,0:T(8,128)(2,1)} %all-gather.2.cloned.1.call-done, bf16[8192,2048]{1,0:T(8,128)(2,1)} %param.12), kind=kOutput, calls=%fused_computation.83 | convolution fusion | flops 4294967296 | bytes 36700160 | tf_op jit(solution)/shard_map/dot_general | solution.py:127
  150.2 27.6 %reduce-scatter.2.cloned.1.call-done = bf16[2048,128]{0,1:T(8,128)(2,1)} async-done(((bf16[8192,128]{0,1:T(8,128)(2,1)}), bf16[2048,128]{0,1:T(8,128)(2,1)}) %reduce-scatter.2.cloned.1.call-update) | async-done | bytes 524304 | tf_op jit(solution)/shard_map/reduce_scatter | solution.py:106
  177.8 3.8 %fusion.5 = (bf16[128,2048]{1,0:T(8,128)(2,1)}, bf16[128,2048]{1,0:T(8,128)(2,1)}) fusion(bf16[2048,128]{0,1:T(8,128)(2,1)} %reduce-scatter.2.cloned.1.call-done, bf16[128,2048]{1,0:T(8,128)(2,1)} %collective-permute-done.11, bf16[128,2048]{1,0:T(8,128)(2,1)} %collective-permute-done.9, bf16[512,2048]{1,0:T(8,128)(2,1)S(1)} %convolution_convert_fusion.1, ...), kind=kLoop, calls=%fused_computation.16 | loop fusion | flops 3407872 | bytes 5767680 | tf_op jit(solution)/shard_map/convert_element_type | solution.py:159
  (65 shorter events, 6.0 us)
Async XLA Ops:
  7.2 32.6 %copy-start = (bf16[1,2048,256]{2,1,0:T(8,128)(2,1)S(1)}, bf16[1,2048,256]{2,1,0:T(8,128)(2,1)}, u32[]{:S(2)}) copy-start(bf16[1,2048,256]{2,1,0:T(8,128)(2,1)} %param.13) | copy-start | bytes 3145732
  7.2 78.2 %all-reduce.3.cloned.1.call-start = ((), (), s32[]{:S(2)}) async-start(), calls=%async_computation.3 | async-start | bytes 1048576 | tf_op jit(solution)/shard_map/psum | solution.py:133
  7.2 16.1 %collective-permute-start = (bf16[128,2048]{1,0:T(8,128)(2,1)}, bf16[128,2048]{1,0:T(8,128)(2,1)}, u32[]{:S(2)}, u32[]{:S(2)}) collective-permute-start(bf16[128,2048]{1,0:T(8,128)(2,1)} %param.11), channel_id=1, source_target_pairs={{0,2},{1,3},{2,0},{3,1},{4,6},{5,7},{6,4},{7,5},{8,10},{9,11},{10,... | collective-permute-start | bytes 1572872 | tf_op jit(solution)/shard_map/ppermute | solution.py:13
  10.2 26.4 %collective-permute-start.1 = (bf16[128,2048]{1,0:T(8,128)(2,1)}, bf16[128,2048]{1,0:T(8,128)(2,1)}, u32[]{:S(2)}, u32[]{:S(2)}) collective-permute-start(bf16[128,2048]{1,0:T(8,128)(2,1)} %param.11), channel_id=1, source_target_pairs={{0,1},{1,0},{2,3},{3,2},{4,5},{5,4},{6,7},{7,6},{8,9},{9,8},{10,11... | collective-permute-start | bytes 1572872 | tf_op jit(solution)/shard_map/ppermute | solution.py:13
  10.2 23.5 %collective-permute-start.6 = (bf16[128,2048]{1,0:T(8,128)(2,1)}, bf16[128,2048]{1,0:T(8,128)(2,1)}, u32[]{:S(2)}, u32[]{:S(2)}) collective-permute-start(bf16[128,2048]{1,0:T(8,128)(2,1)} %param.15), channel_id=1, source_target_pairs={{0,2},{1,3},{2,0},{3,1},{4,6},{5,7},{6,4},{7,5},{8,10},{9,11},{10,... | collective-permute-start | bytes 1572872 | tf_op jit(solution)/shard_map/ppermute | solution.py:13
  10.4 27.4 %collective-permute-start.7 = (bf16[128,2048]{1,0:T(8,128)(2,1)}, bf16[128,2048]{1,0:T(8,128)(2,1)}, u32[]{:S(2)}, u32[]{:S(2)}) collective-permute-start(bf16[128,2048]{1,0:T(8,128)(2,1)} %param.15), channel_id=1, source_target_pairs={{0,1},{1,0},{2,3},{3,2},{4,5},{5,4},{6,7},{7,6},{8,9},{9,8},{10,11... | collective-permute-start | bytes 1572872 | tf_op jit(solution)/shard_map/ppermute | solution.py:13
  23.3 16.4 %collective-permute-start.2 = (bf16[128,2048]{1,0:T(8,128)(2,1)}, bf16[128,2048]{1,0:T(8,128)(2,1)S(1)}, u32[]{:S(2)}, u32[]{:S(2)}) collective-permute-start(bf16[128,2048]{1,0:T(8,128)(2,1)} %collective-permute-done), channel_id=1, source_target_pairs={{0,1},{1,0},{2,3},{3,2},{4,5},{5,4},{6,7},{7,6},{8,9},{9,8},{10,11... | collective-permute-start | bytes 1572872 | tf_op jit(solution)/shard_map/ppermute | solution.py:13
  33.7 7.5 %collective-permute-start.8 = (bf16[128,2048]{1,0:T(8,128)(2,1)}, bf16[128,2048]{1,0:T(8,128)(2,1)S(1)}, u32[]{:S(2)}, u32[]{:S(2)}) collective-permute-start(bf16[128,2048]{1,0:T(8,128)(2,1)} %collective-permute-done.6), channel_id=1, source_target_pairs={{0,1},{1,0},{2,3},{3,2},{4,5},{5,4},{6,7},{7,6},{8,9},{9,8},{10,11... | collective-permute-start | bytes 1572872 | tf_op jit(solution)/shard_map/ppermute | solution.py:13
  39.7 5.6 %copy-start.2 = (bf16[512,2048]{1,0:T(8,128)(2,1)}, bf16[512,2048]{1,0:T(8,128)(2,1)S(1)}, u32[]{:S(2)}) copy-start(bf16[512,2048]{1,0:T(8,128)(2,1)S(1)} %constant_dynamic-update-slice_fusion) | copy-start | bytes 6291460
  39.8 2.4 %copy-start.3 = (bf16[512,2048]{1,0:T(8,128)(2,1)S(1)}, bf16[512,2048]{1,0:T(8,128)(2,1)}, u32[]{:S(2)}) copy-start(bf16[512,2048]{1,0:T(8,128)(2,1)} %constant_dynamic-update-slice_fusion.5) | copy-start | bytes 6291460
  39.8 3.8 %copy-start.5 = (bf16[1,256,2048]{2,1,0:T(8,128)(2,1)S(1)}, bf16[1,256,2048]{2,1,0:T(8,128)(2,1)}, u32[]{:S(2)}) copy-start(bf16[1,256,2048]{2,1,0:T(8,128)(2,1)} %param.14) | copy-start | bytes 3145732
  42.2 1.4 copy-start.4
  45.1 87.8 %all-gather.2.cloned.1.call-start = ((), (), s32[]{:S(2)}) async-start(), calls=%async_computation.1 | async-start | bytes 2621440 | tf_op jit(solution)/shard_map/all_gather | solution.py:126
  46.6 131.1 %reduce-scatter.2.cloned.1.call-start = ((), (), s32[]{:S(2)}) async-start(), calls=%async_computation.2 | async-start | bytes 2621440 | tf_op jit(solution)/shard_map/reduce_scatter | solution.py:106
  70.0 1.4 copy-start.7
  86.7 2.9 %copy-start.6 = (bf16[1,256,2048]{2,1,0:T(8,128)(2,1)S(1)}, bf16[1,256,2048]{2,1,0:T(8,128)(2,1)}, u32[]{:S(2)}) copy-start(bf16[1,256,2048]{2,1,0:T(8,128)(2,1)} %param.14) | copy-start | bytes 3145732
  89.5 11.6 %collective-permute-start.10 = (bf16[128,2048]{1,0:T(8,128)(2,1)}, bf16[128,2048]{1,0:T(8,128)(2,1)}, u32[]{:S(2)}, u32[]{:S(2)}) collective-permute-start(bf16[128,2048]{1,0:T(8,128)(2,1)} %get-tuple-element.12), channel_id=1, source_target_pairs={{0,1},{1,0},{2,3},{3,2},{4,5},{5,4},{6,7},{7,6},{8,9},{9,8},{10,11... | collective-permute-start | bytes 1572872 | tf_op jit(solution)/shard_map/ppermute | solution.py:13
  90.3 1.3 copy-start.1
  92.7 11.8 %collective-permute-start.4 = (bf16[128,2048]{1,0:T(8,128)(2,1)}, bf16[128,2048]{1,0:T(8,128)(2,1)}, u32[]{:S(2)}, u32[]{:S(2)}) collective-permute-start(bf16[128,2048]{1,0:T(8,128)(2,1)} %get-tuple-element.14), channel_id=1, source_target_pairs={{0,1},{1,0},{2,3},{3,2},{4,5},{5,4},{6,7},{7,6},{8,9},{9,8},{10,11... | collective-permute-start | bytes 1572872 | tf_op jit(solution)/shard_map/ppermute | solution.py:13
  100.6 49.6 %collective-permute-start.9 = (bf16[128,2048]{1,0:T(8,128)(2,1)}, bf16[128,2048]{1,0:T(8,128)(2,1)}, u32[]{:S(2)}, u32[]{:S(2)}) collective-permute-start(bf16[128,2048]{1,0:T(8,128)(2,1)} %get-tuple-element.11), channel_id=1, source_target_pairs={{0,1},{1,0},{2,3},{3,2},{4,5},{5,4},{6,7},{7,6},{8,9},{9,8},{10,11... | collective-permute-start | bytes 1572872 | tf_op jit(solution)/shard_map/ppermute | solution.py:13
  100.6 49.6 %collective-permute-start.3 = (bf16[128,2048]{1,0:T(8,128)(2,1)}, bf16[128,2048]{1,0:T(8,128)(2,1)}, u32[]{:S(2)}, u32[]{:S(2)}) collective-permute-start(bf16[128,2048]{1,0:T(8,128)(2,1)} %get-tuple-element.13), channel_id=1, source_target_pairs={{0,1},{1,0},{2,3},{3,2},{4,5},{5,4},{6,7},{7,6},{8,9},{9,8},{10,11... | collective-permute-start | bytes 1572872 | tf_op jit(solution)/shard_map/ppermute | solution.py:13
  103.0 47.2 %collective-permute-start.11 = (bf16[128,2048]{1,0:T(8,128)(2,1)}, bf16[128,2048]{1,0:T(8,128)(2,1)}, u32[]{:S(2)}, u32[]{:S(2)}) collective-permute-start(bf16[128,2048]{1,0:T(8,128)(2,1)} %slice_add_fusion), channel_id=1, source_target_pairs={{0,2},{1,3},{2,0},{3,1},{4,6},{5,7},{6,4},{7,5},{8,10},{9,11},{10,... | collective-permute-start | bytes 1572872 | tf_op jit(solution)/shard_map/ppermute | solution.py:13
  106.6 43.6 %collective-permute-start.5 = (bf16[128,2048]{1,0:T(8,128)(2,1)}, bf16[128,2048]{1,0:T(8,128)(2,1)}, u32[]{:S(2)}, u32[]{:S(2)}) collective-permute-start(bf16[128,2048]{1,0:T(8,128)(2,1)} %slice_add_fusion.2), channel_id=1, source_target_pairs={{0,2},{1,3},{2,0},{3,1},{4,6},{5,7},{6,4},{7,5},{8,10},{9,11},{10,... | collective-permute-start | bytes 1572872 | tf_op jit(solution)/shard_map/ppermute | solution.py:13
Sparse Core Ops, SparseCore 0:
  45.2 40.1 all-reduce.2
  86.9 45.9 all-gather.1
  135.2 42.5 reduce-scatter.1
where the time goes:
time: 189 us; the launch traced here: 188 us
  waiting for transfers between devices  82.6 us (44%)
  matrix products  55.8 us (30%)
  local copies, waits for them, and re-layouts  15.6 us (8%)
  between operations  15.3 us (8%)
  other arithmetic  12 us (6%)
  starting transfers between devices  6.87 us (4%)
    reduce_scatter x1, waiting for transfers between devices, local(): lax.psum_scatter(back_part, 'tensor', scatter_dimension=0, tiled=True)  27.6 us
    all_gather x1, waiting for transfers between devices, local(): x_full = lax.all_gather(x_own, 'tensor', axis=1, tiled=True)  25.8 us
    dot_general x1, matrix products, local(): lax.dot_general(weight, cotangent, (((1,), (1,)), ((), ())), preferred_el...  23.2 us
    dot_general x1, matrix products, local(): base = jnp.dot(x_full, weight, preferred_element_type=f32)  17.3 us
    ppermute x12, waiting for transfers between devices, swap(): return lax.ppermute(value, 'dp', [(i, i ^ bit) for i in range(n)])  15.7 us
    psum x1, waiting for transfers between devices, local(): u_sum, g_sum = (lax.psum(u_part, 'tensor'), lax.psum(g_part, 'tensor'))  13.4 us
    unnamed x22, local copies, waits for them, and re-layouts  12.6 us
    ppermute x12, starting transfers between devices, swap(): return lax.ppermute(value, 'dp', [(i, i ^ bit) for i in range(n)])  6.57 us
  transfers between devices with their start and end apart: 15, of which 5 were waited for; matrix products, arithmetic and copies ran while one was open for 40% of the time, Pallas kernels for 0%

commit v1 on v0

--- a/solution.py
+++ b/solution.py
@@ -1,6 +1,8 @@
 import jax
 import jax.numpy as jnp
 from jax import lax
+from jax.experimental import pallas as pl
+from jax.experimental.pallas import tpu as pltpu
 from jax.sharding import PartitionSpec as P
 
 RANK_LOW = 16
@@ -74,7 +76,397 @@
     table_ids = jnp.arange(adapter_home_row.shape[0], dtype=jnp.int32)
     matches = (adapter[:, None] == table_ids[None, :]).astype(jnp.int32)
     home = jnp.sum(matches * adapter_home_row[None, :], axis=1)
-    return micro_target, slot_ids, home, counted
+    micro_matches = (micro_adapter[:, None] == table_ids[None, :]).astype(jnp.int32)
+    micro_home = jnp.sum(micro_matches * adapter_home_row[None, :], axis=1)
+    micro_home = jnp.sum(here * micro_home[None, :], axis=1)
+    return micro_target, micro_home, slot_ids, home, counted
+
+
+def layer_kernel(
+    tokens, cotangent, weight, down, up, move, micro_mine, mine, own_live, columns, scale,
+    outputs, input_gradient, grad_a, grad_b,
+    x_all, dy_all, gathered, part, up_got, down_got, up_sum, down_sum, blocks,
+    narrow, narrow_pair, narrow_sum, narrow_peer, narrow_own, narrow_got, narrow_all,
+    out_delta, out_pair, out_sum, out_peer, back_delta, back_pair, back_sum, back_peer,
+    base, load_sem, send_sem, recv_sem,
+):
+    f32, bf16 = jnp.float32, jnp.bfloat16
+    me, spot = lax.axis_index("dp"), lax.axis_index("tensor")
+    core_peer = me + 1 - 2 * lax.rem(me, 2)
+    chip_peer = lax.rem(me + 2, 4)
+    rows, features = tokens.shape
+    rank = down.shape[1]
+    tile = 256
+    low_half = spot < 2
+    far_index = jnp.where(low_half, lax.rem(spot + 3, 4), lax.rem(spot + 1, 4))
+    middle_index = lax.rem(spot + 2, 4)
+    near_index = jnp.where(low_half, spot + 1, spot - 1)
+    FAR, MIDDLE, NEAR, OWN = 0, 1, 2, 3
+    count = [0]
+
+    def remote(src, dst, target):
+        k = count[0]
+        count[0] += 1
+        return pltpu.make_async_remote_copy(
+            src_ref=src, dst_ref=dst, send_sem=send_sem.at[k], recv_sem=recv_sem.at[k],
+            device_id=target, device_id_type=pl.DeviceIdType.MESH,
+        )
+
+    def load(k, slot, index):
+        start = pl.multiple_of(index * features, features)
+        return pltpu.make_async_copy(
+            weight.at[pl.ds(start, features), :], blocks.at[slot], load_sem.at[k]
+        )
+
+    def tiles(size, body):
+        @pl.loop(0, size // tile)
+        def _(i):
+            body(pl.ds(pl.multiple_of(i * tile, tile), tile))
+
+    def nn(a, b):
+        return jnp.dot(a, b, preferred_element_type=f32)
+
+    def nt(a, b):
+        return lax.dot_general(a, b, (((1,), (1,)), ((), ())), preferred_element_type=f32)
+
+    far_load, middle_load = load(0, 0, far_index), load(1, 1, middle_index)
+    near_load, own_load = load(2, 2, near_index), load(3, 0, spot)
+    again_load = load(4, 2, far_index)
+    for copy in (far_load, middle_load, near_load):
+        copy.start()
+
+    barrier = pltpu.get_barrier_semaphore()
+    partners = [{"dp": core_peer}, {"dp": chip_peer}]
+    partners += [{"tensor": lax.rem(spot + k, 4)} for k in (1, 2, 3)]
+    for partner in partners:
+        pl.semaphore_signal(barrier, inc=1, device_id=partner, device_id_type=pl.DeviceIdType.MESH)
+    pl.semaphore_wait(barrier, len(partners))
+
+    chip, core = {"dp": chip_peer}, {"dp": core_peer}
+    above, below = {"tensor": lax.rem(spot + 1, 4)}, {"tensor": lax.rem(spot + 3, 4)}
+
+    def block(ref, j):
+        return ref.at[pl.ds(j * rows, rows), :]
+
+    x_chip = remote(tokens, block(x_all, 1), chip)
+    x_core = remote(tokens, block(x_all, 2), core)
+    x_last = remote(block(x_all, 1), block(x_all, 3), core)
+    dy_chip = remote(cotangent, block(dy_all, 1), chip)
+    dy_core = remote(cotangent, block(dy_all, 2), core)
+    dy_last = remote(block(dy_all, 1), block(dy_all, 3), core)
+    x_chip.start()
+    x_core.start()
+    dy_chip.start()
+    dy_core.start()
+    x_all[0:rows, :] = tokens[...]
+    dy_all[0:rows, :] = cotangent[...]
+
+    def backward(which, slot):
+        def body(at):
+            part[which, :, at] = nt(cotangent[...], blocks[slot, at, :]).astype(bf16)
+
+        tiles(features, body)
+
+    def forward(index, slot, first=False):
+        def body(at):
+            term = nn(gathered[index], blocks[slot, :, at])
+            base[:, at] = term if first else base[:, at] + term
+
+        tiles(features, body)
+
+    def add(target, a, b):
+        def body(at):
+            target[:, at] = (a[:, at].astype(f32) + b[:, at].astype(f32)).astype(bf16)
+
+        tiles(target.shape[1], body)
+
+    up_far = remote(part.at[FAR], up_got.at[0], above)
+    down_far = remote(part.at[FAR], down_got.at[0], below)
+    up_middle = remote(up_sum.at[0], up_got.at[1], above)
+    down_middle = remote(down_sum.at[0], down_got.at[1], below)
+    up_near = remote(up_sum.at[1], up_got.at[2], above)
+    down_near = remote(down_sum.at[1], down_got.at[2], below)
+    up_gather = [
+        remote(gathered.at[lax.rem(spot + 4 - k, 4)], gathered.at[lax.rem(spot + 4 - k, 4)], above)
+        for k in range(3)
+    ]
+    down_gather = [
+        remote(gathered.at[lax.rem(spot + k, 4)], gathered.at[lax.rem(spot + k, 4)], below)
+        for k in range(3)
+    ]
+
+    far_load.wait()
+    backward(FAR, 0)
+    pl.when(spot == 0)(up_far.start)
+    pl.when(spot == 3)(down_far.start)
+    own_load.start()
+    x_chip.wait_recv()
+    x_last.start()
+
+    middle_load.wait()
+    backward(MIDDLE, 1)
+
+    @pl.when(spot == 0)
+    def _():
+        up_sum[0] = part[MIDDLE]
+        up_middle.start()
+
+    @pl.when(spot == 3)
+    def _():
+        down_sum[0] = part[MIDDLE]
+        down_middle.start()
+
+    x_core.wait_recv()
+    x_last.wait_recv()
+
+    def pack(at):
+        gathered[spot, :, at] = nn(move[0:rows, :], x_all[:, at]).astype(bf16)
+
+    tiles(features, pack)
+    pl.when(spot < 3)(up_gather[0].start)
+    pl.when(spot > 0)(down_gather[0].start)
+    narrow[:, 0:rank] = (nn(x_all[...], down[...]) * micro_mine[...]).astype(bf16)
+
+    near_load.wait()
+    backward(NEAR, 2)
+    dy_chip.wait_recv()
+    dy_last.start()
+
+    @pl.when(spot == 1)
+    def _():
+        up_far.wait_recv()
+        add(up_sum.at[0], part.at[MIDDLE], up_got.at[0])
+        up_middle.start()
+
+    @pl.when(spot == 2)
+    def _():
+        down_far.wait_recv()
+        add(down_sum.at[0], part.at[MIDDLE], down_got.at[0])
+        down_middle.start()
+
+    dy_core.wait_recv()
+    dy_last.wait_recv()
+    narrow[:, rank : 2 * rank] = (nt(dy_all[...], up[...]) * mine[...]).astype(bf16)
+    pair = remote(narrow.at[pl.ds(2 * rows, 2 * rows), :], narrow_pair, core)
+    pair.start()
+    own_load.wait()
+    backward(OWN, 0)
+
+    @pl.when(spot == 0)
+    def _():
+        up_sum[1] = part[NEAR]
+        up_near.start()
+
+    @pl.when(spot == 3)
+    def _():
+        down_sum[1] = part[NEAR]
+        down_near.start()
+
+    pair.wait_recv()
+    narrow_sum[...] = narrow[rows : 2 * rows, :] + narrow_pair[rows : 2 * rows, :]
+    peer = remote(narrow_sum, narrow_peer, chip)
+    peer.start()
+    forward(spot, 0, first=True)
+
+    peer.wait_recv()
+    narrow_own[...] = narrow[0:rows, :] + narrow_pair[0:rows, :] + narrow_peer[...]
+    spread = [
+        remote(narrow_own, narrow_got.at[k - 1], {"tensor": lax.rem(spot + k, 4)})
+        for k in (1, 2, 3)
+    ]
+    for copy in spread:
+        copy.start()
+
+    @pl.when((spot == 1) | (spot == 2))
+    def _():
+        up_middle.wait_recv()
+        down_middle.wait_recv()
+
+    @pl.when(spot == 1)
+    def _():
+        add(up_sum.at[1], part.at[NEAR], up_got.at[1])
+        add(down_sum.at[1], part.at[FAR], down_got.at[1])
+        up_near.start()
+        down_near.start()
+
+    @pl.when(spot == 2)
+    def _():
+        add(up_sum.at[1], part.at[FAR], up_got.at[1])
+        add(down_sum.at[1], part.at[NEAR], down_got.at[1])
+        up_near.start()
+        down_near.start()
+
+    def pass_on(k):
+        @pl.when(spot >= k)
+        def _():
+            up_gather[k - 1].wait_recv()
+
+        @pl.when(spot <= 3 - k)
+        def _():
+            down_gather[k - 1].wait_recv()
+
+        if k < 3:
+            pl.when((spot >= k) & (spot < 3))(up_gather[k].start)
+            pl.when((spot <= 3 - k) & (spot > 0))(down_gather[k].start)
+
+    pass_on(1)
+    forward(near_index, 2)
+    again_load.start()
+
+    for copy in spread:
+        copy.wait_recv()
+    total = narrow_own[...].astype(f32)
+    for k in range(3):
+        total = total + narrow_got[k].astype(f32)
+    narrow_all[0:rows, :] = total.astype(bf16)
+    all_chip = remote(block(narrow_all, 0), block(narrow_all, 1), chip)
+    all_core = remote(block(narrow_all, 0), block(narrow_all, 2), core)
+    all_last = remote(block(narrow_all, 1), block(narrow_all, 3), core)
+    all_chip.start()
+    all_core.start()
+    all_chip.wait_recv()
+    all_last.start()
+    pass_on(2)
+    all_core.wait_recv()
+    all_last.wait_recv()
+
+    low_source = (narrow_all[:, 0:rank].astype(f32) * columns[...]).astype(bf16)
+    low_wide = nn(move[...], low_source) * mine[...]
+    low = low_wide.astype(bf16)
+    factor = columns[...] * scale[...]
+    grad_low_wide = narrow_all[:, rank : 2 * rank].astype(f32) * factor * mine[...]
+    grad_low = grad_low_wide.astype(bf16)
+
+    def deltas(at):
+        out_delta[:, at] = (scale[...] * nn(low, up[:, at])).astype(bf16)
+        back_delta[:, at] = nt(grad_low, down[at, :]).astype(bf16)
+
+    tiles(features, deltas)
+    second = pl.ds(2 * rows, 2 * rows)
+    out_core = remote(out_delta.at[second, :], out_pair, core)
+    back_core = remote(back_delta.at[second, :], back_pair, core)
+    out_core.start()
+    back_core.start()
+    forward(middle_index, 1)
+    out_core.wait_recv()
+    add(out_sum, block(out_delta, 1), block(out_pair, 1))
+    out_chip = remote(out_sum, out_peer, chip)
+    out_chip.start()
+    back_core.wait_recv()
+    add(back_sum, block(back_delta, 1), block(back_pair, 1))
+    back_chip = remote(back_sum, back_peer, chip)
+    back_chip.start()
+
+    low_turned = low_wide.T.astype(bf16)
+    grad_turned = nn(grad_low_wide.T.astype(bf16), move[...]).astype(bf16)
+
+    def gradients(at):
+        grad_b[:, at] = (scale[...] * nn(low_turned, dy_all[:, at])).astype(bf16)
+        grad_a[at, :] = nn(grad_turned, x_all[:, at]).T.astype(bf16)
+
+    tiles(features, gradients)
+    pass_on(3)
+    again_load.wait()
+    forward(far_index, 2)
+    out_chip.wait_recv()
+
+    def finish_out(at):
+        delta = out_delta[0:rows, at].astype(f32) + out_pair[0:rows, at].astype(f32)
+        delta = delta + out_peer[:, at].astype(f32)
+        outputs[:, at] = (own_live[...] * (base[:, at] + delta)).astype(bf16)
+
+    tiles(features, finish_out)
+    base[...] = part[OWN].astype(f32)
+
+    @pl.when(spot > 0)
+    def _():
+        up_near.wait_recv()
+        base[...] = base[...] + up_got[2].astype(f32)
+
+    @pl.when(spot < 3)
+    def _():
+        down_near.wait_recv()
+        base[...] = base[...] + down_got[2].astype(f32)
+
+    back_chip.wait_recv()
+
+    def finish_back(at):
+        delta = back_delta[0:rows, at].astype(f32) + back_pair[0:rows, at].astype(f32)
+        delta = delta + back_peer[:, at].astype(f32)
+        input_gradient[:, at] = (own_live[...] * (base[:, at] + delta)).astype(bf16)
+
+    tiles(features, finish_back)
+
+    for copy in (x_chip, x_core, x_last, dy_chip, dy_core, dy_last, pair, peer, *spread):
+        copy.wait_send()
+    for copy in (all_chip, all_core, all_last, out_core, out_chip, back_core, back_chip):
+        copy.wait_send()
+    pl.when(spot == 0)(up_far.wait_send)
+    pl.when(spot == 3)(down_far.wait_send)
+    pl.when(spot < 2)(up_middle.wait_send)
+    pl.when(spot >= 2)(down_middle.wait_send)
+    pl.when(spot < 3)(up_near.wait_send)
+    pl.when(spot > 0)(down_near.wait_send)
+    for k in range(3):
+        pl.when((spot >= k) & (spot < 3))(up_gather[k].wait_send)
+        pl.when((spot <= 3 - k) & (spot > 0))(down_gather[k].wait_send)
+
+
+def layer(tokens, cotangent, weight, down, up, *rest):
+    rows, features = tokens.shape
+    rank = down.shape[1]
+    bf16 = jnp.bfloat16
+
+    def held(*shape):
+        return pltpu.VMEM(shape, bf16)
+
+    vmem = pl.BlockSpec(memory_space=pltpu.VMEM)
+    all_rows = 4 * rows
+    return pl.pallas_call(
+        layer_kernel,
+        out_shape=(
+            jax.ShapeDtypeStruct((rows, features), bf16),
+            jax.ShapeDtypeStruct((rows, features), bf16),
+            jax.ShapeDtypeStruct((features, rank), bf16),
+            jax.ShapeDtypeStruct((rank, features), bf16),
+        ),
+        in_specs=[vmem, vmem, pl.BlockSpec(memory_space=pl.ANY)] + [vmem] * (2 + len(rest)),
+        out_specs=(vmem,) * 4,
+        scratch_shapes=[
+            held(all_rows, features),
+            held(all_rows, features),
+            held(4, rows, features),
+            held(4, rows, features),
+            held(3, rows, features),
+            held(3, rows, features),
+            held(2, rows, features),
+            held(2, rows, features),
+            held(3, features, features),
+            held(all_rows, 2 * rank),
+            held(2 * rows, 2 * rank),
+            held(rows, 2 * rank),
+            held(rows, 2 * rank),
+            held(rows, 2 * rank),
+            held(3, rows, 2 * rank),
+            held(all_rows, 2 * rank),
+            held(all_rows, features),
+            held(2 * rows, features),
+            held(rows, features),
+            held(rows, features),
+            held(all_rows, features),
+            held(2 * rows, features),
+            held(rows, features),
+            held(rows, features),
+            pltpu.VMEM((rows, features), jnp.float32),
+            pltpu.SemaphoreType.DMA((5,)),
+            pltpu.SemaphoreType.DMA((40,)),
+            pltpu.SemaphoreType.DMA((40,)),
+        ],
+        compiler_params=pltpu.CompilerParams(
+            collective_id=0, has_side_effects=True, vmem_limit_bytes=60 * 1024 * 1024
+        ),
+        name="layer",
+    )(tokens, cotangent, weight, down, up, *rest)
 
 
 def local(
@@ -97,30 +489,38 @@
     f32, bf16 = jnp.float32, jnp.bfloat16
     down, up = adapter_down_factor[0], adapter_up_factor[0]
 
-    x_all = gather_blocks(tokens, n)
-    dy_all = gather_blocks(cotangent, n)
-
-    back_part = lax.dot_general(
-        weight, cotangent, (((1,), (1,)), ((), ())), preferred_element_type=f32
-    ).astype(bf16)
-    back = lax.psum_scatter(back_part, "tensor", scatter_dimension=0, tiled=True).T
-
-    micro_target, slot_ids, home, counted = packing(
+    micro_target, micro_home, slot_ids, home, counted = packing(
         micro_destination_group, micro_adapter, micro_token_count, adapter_home_row, n, me
     )
-    token = jnp.arange(x_all.shape[0], dtype=jnp.int32) % MICRO_TOKENS
-    place = jnp.arange(dy_all.shape[0], dtype=jnp.int32) % MICRO_TOKENS
+    token = jnp.arange(tokens.shape[0] * n, dtype=jnp.int32) % MICRO_TOKENS
+    place = jnp.arange(own_rows * n, dtype=jnp.int32) % MICRO_TOKENS
     move = (
         (rows_of(slot_ids) * MICRO_TOKENS + place)[:, None]
         == (rows_of(micro_target) * MICRO_TOKENS + token)[None, :]
     ).astype(bf16)
     live = place < rows_of(counted)
     mine = (live & (rows_of(home) == me)).astype(f32)[:, None]
+    micro_mine = (rows_of(micro_home) == me).astype(f32)[:, None]
     own_live = live[:own_rows].astype(f32)[:, None]
     bucket = jnp.sum(jnp.where(adapter_home_row == me, adapter_rank_bucket, 0))
     rank = RANK_LOW * jnp.where(bucket == 0, 1, jnp.where(bucket == 1, 4, 16))
     scale = jnp.sqrt(LARGEST_RANK / rank.astype(f32))
     columns = (jnp.arange(LARGEST_RANK, dtype=jnp.int32) < rank).astype(f32)[None, :]
+
+    if n == 4 and n_tensor == 4 and tokens.shape == cotangent.shape:
+        outputs, input_gradient, grad_a, grad_b = layer(
+            tokens, cotangent, weight, down, up, move, micro_mine, mine, own_live, columns,
+            scale.reshape(1, 1),
+        )
+        return outputs, input_gradient, grad_a[None], grad_b[None]
+
+    x_all = gather_blocks(tokens, n)
+    dy_all = gather_blocks(cotangent, n)
+
+    back_part = lax.dot_general(
+        weight, cotangent, (((1,), (1,)), ((), ())), preferred_element_type=f32
+    ).astype(bf16)
+    back = lax.psum_scatter(back_part, "tensor", scatter_dimension=0, tiled=True).T
 
     x_own = jnp.dot(move[:own_rows], x_all, preferred_element_type=f32).astype(bf16)
     x_full = lax.all_gather(x_own, "tensor", axis=1, tiled=True)

time: 189 us -> 134 us (0.71)
  the two profiles are of different devices: /device:TPU:0 before, /device:TPU:10 now
where the time goes in v1:
time: 134 us
  Pallas kernels  113 us (84%)
  local copies, waits for them, and re-layouts  11.1 us (8%)
  other arithmetic  7.78 us (6%)
  between operations  2.09 us (2%)
    pallas_call x1, Pallas kernels, layer(): pl.pallas_call(layer_kernel, out_shape=(jax.ShapeDtypeStruct((rows, featu...  113 us
    unnamed x4, local copies, waits for them, and re-layouts  8.33 us

profile of v1, /device:TPU:10, one launch (start us, length us, event | category | flops | bytes accessed | tf_op | source)
XLA Modules:
  0.0 133.8 jit_solution(16392636328708552450)
XLA Ops:
  0.6 1.3 fusion.11
  3.3 0.7 xor_multiply_fusion
  4.0 0.6 compare_convert_fusion.1.columns
  4.6 0.9 convert_reduce_fusion
  5.5 0.7 add_add_fusion
  6.2 0.1 iota_add_fusion
  6.2 0.1 add.99
  6.3 0.9 fusion.1
  7.2 0.8 select_reduce_fusion.2
  8.0 0.2 select_reduce_fusion
  8.2 0.1 broadcast_in_dim.25
  8.3 0.1 broadcast_in_dim.23
  8.3 0.1 broadcast_in_dim.22
  8.4 0.1 mul.106
  8.5 0.1 broadcast_in_dim.21
  8.5 0.1 mul.98
  8.6 0.1 broadcast_in_dim.24
  8.7 0.1 reshape.188
  8.8 0.1 reshape.187
  8.9 0.2 eq.159
  9.1 0.2 copy.24
  9.3 0.7 copy.27.own_live
  10.1 0.7 and_convert_fusion.mine
  10.8 0.9 convert_element_type.55.micro_mine
  11.7 0.9 compare_convert_fusion.move
  12.6 112.9 %layer.1 = (bf16[128,2048]{1,0:T(8,128)(2,1)}, bf16[128,2048]{1,0:T(8,128)(2,1)}, bf16[2048,256]{1,0:T(8,128)(2,1)}, bf16[256,2048]{1,0:T(8,128)(2,1)}) custom-call(bf16[128,2048]{1,0:T(8,128)(2,1)} %tokens.1, bf16[128,2048]{1,0:T(8,128)(2,1)} %cotangent.1, bf16[8192,2048]{1,0:T(8,128)(2,1)} %weight.1, bf16[2048,256]{1,0:T(8,128)(2,1)} %bitcast.9, ...), custom_call_target="tpu_custom_call" | custom-call | tf_op jit(solution)/shard_map/layer/pallas_call | solution.py:425
  125.5 1.9 %copy.32 = bf16[128,2048]{1,0:T(8,128)(2,1)} copy(bf16[128,2048]{1,0:T(8,128)(2,1)} %get-tuple-element.25) | data formatting | bytes 1048576
  127.4 1.9 %copy.33 = bf16[128,2048]{1,0:T(8,128)(2,1)} copy(bf16[128,2048]{1,0:T(8,128)(2,1)} %get-tuple-element.26) | data formatting | bytes 1048576
  129.2 2.3 %copy.34 = bf16[1,2048,256]{2,1,0:T(8,128)(2,1)} copy(bf16[1,2048,256]{2,1,0:T(8,128)(2,1)} %bitcast.12) | data formatting | bytes 2097152
  131.5 2.3 %copy.35 = bf16[1,256,2048]{2,1,0:T(8,128)(2,1)} copy(bf16[1,256,2048]{2,1,0:T(8,128)(2,1)} %bitcast.11) | data formatting | bytes 2097152
  (8 shorter events, 0.1 us)

commit v2 on v1

--- a/solution.py
+++ b/solution.py
@@ -1,3 +1,5 @@
+import functools
+
 import jax
 import jax.numpy as jnp
 from jax import lax
@@ -83,10 +85,10 @@
 
 
 def layer_kernel(
-    tokens, cotangent, weight, down, up, move, micro_mine, mine, own_live, columns, scale,
+    tokens, cotangent, weight, down, up, destination, adapter, live_count, bucket, home_row,
     outputs, input_gradient, grad_a, grad_b,
     x_all, dy_all, gathered, part, up_got, down_got, up_sum, down_sum, blocks,
-    narrow, narrow_pair, narrow_sum, narrow_peer, narrow_own, narrow_got, narrow_all,
+    move, narrow, narrow_pair, narrow_sum, narrow_peer, narrow_own, narrow_got, narrow_all,
     out_delta, out_pair, out_sum, out_peer, back_delta, back_pair, back_sum, back_peer,
     base, load_sem, send_sem, recv_sem,
 ):
@@ -156,7 +158,6 @@
     dy_last = remote(block(dy_all, 1), block(dy_all, 3), core)
     x_chip.start()
     x_core.start()
-    dy_chip.start()
     dy_core.start()
     x_all[0:rows, :] = tokens[...]
     dy_all[0:rows, :] = cotangent[...]
@@ -195,27 +196,139 @@
         for k in range(3)
     ]
 
+    def exchange(kind):
+        sides = narrow.at[kind], narrow_pair.at[kind], narrow_all.at[kind]
+        pair = remote(sides[0].at[pl.ds(2 * rows, 2 * rows), :], sides[1], core)
+        peer = remote(narrow_sum.at[kind], narrow_peer.at[kind], chip)
+        spread = [
+            remote(narrow_own.at[kind], narrow_got.at[kind, k - 1], {"tensor": lax.rem(spot + k, 4)})
+            for k in (1, 2, 3)
+        ]
+        all_chip = remote(block(sides[2], 0), block(sides[2], 1), chip)
+        all_core = remote(block(sides[2], 0), block(sides[2], 2), core)
+        all_last = remote(block(sides[2], 1), block(sides[2], 3), core)
+        return pair, peer, spread, all_chip, all_core, all_last
+
+    def send_peer(kind, steps):
+        pair, peer = steps[:2]
+        pair.wait_recv()
+        narrow_sum[kind] = narrow[kind, rows : 2 * rows, :] + narrow_pair[kind, rows : 2 * rows, :]
+        peer.start()
+
+    def send_spread(kind, steps):
+        peer, spread = steps[1:3]
+        peer.wait_recv()
+        narrow_own[kind] = (
+            narrow[kind, 0:rows, :] + narrow_pair[kind, 0:rows, :] + narrow_peer[kind]
+        )
+        for copy in spread:
+            copy.start()
+
+    def send_total(kind, steps):
+        _, _, spread, all_chip, all_core, _ = steps
+        for copy in spread:
+            copy.wait_recv()
+        total = narrow_own[kind].astype(f32)
+        for k in range(3):
+            total = total + narrow_got[kind, k].astype(f32)
+        narrow_all[kind, 0:rows, :] = total.astype(bf16)
+        all_chip.start()
+        all_core.start()
+
+    def send_last(steps):
+        steps[3].wait_recv()
+        steps[5].start()
+
+    def wait_all(steps):
+        steps[4].wait_recv()
+        steps[5].wait_recv()
+
+    def pass_on(k):
+        @pl.when(spot >= k)
+        def _():
+            up_gather[k - 1].wait_recv()
+
+        @pl.when(spot <= 3 - k)
+        def _():
+            down_gather[k - 1].wait_recv()
+
+        if k < 3:
+            pl.when((spot >= k) & (spot < 3))(up_gather[k].start)
+            pl.when((spot <= 3 - k) & (spot > 0))(down_gather[k].start)
+
+    u_steps, g_steps = exchange(0), exchange(1)
+    second = pl.ds(2 * rows, 2 * rows)
+    out_core = remote(out_delta.at[second, :], out_pair, core)
+    back_core = remote(back_delta.at[second, :], back_pair, core)
+    out_chip = remote(out_sum, out_peer, chip)
+    back_chip = remote(back_sum, back_peer, chip)
+
     far_load.wait()
     backward(FAR, 0)
     pl.when(spot == 0)(up_far.start)
     pl.when(spot == 3)(down_far.start)
     own_load.start()
+
+    def iota(shape, axis):
+        return lax.broadcasted_iota(jnp.int32, shape, axis)
+
+    def total_of(mask, values, axis):
+        return jnp.sum(jnp.where(mask, values, 0.0), axis=axis, keepdims=True)
+
+    micros = destination.shape[0]
+    per_group = micros // 4
+    width = 4 * rows
+    first, later = iota((micros, micros), 0), iota((micros, micros), 1)
+    to_column = destination[...].astype(f32)
+    to_row = total_of(first == later, to_column, 0)
+    shares = (first // per_group == later // per_group) & (to_column == to_row)
+    place_column = total_of(shares & (later < first), 1.0, 1)
+    place_row = total_of(shares & (first < later), 1.0, 0)
+    source_column = (iota((micros, 1), 0) // per_group * CAP).astype(f32)
+    source_row = (iota((1, micros), 1) // per_group * CAP).astype(f32)
+    target_column = to_column * (4.0 * CAP) + source_column + place_column
+    target_row = to_row * (4.0 * CAP) + source_row + place_row
+    last_peer = lax.rem(core_peer + 2, 4)
+
+    def unit(index):
+        j = index // rows
+        peer = jnp.where(
+            j == 0, me, jnp.where(j == 1, chip_peer, jnp.where(j == 2, core_peer, last_peer))
+        )
+        return peer * (rows // MICRO_TOKENS) + lax.rem(index, rows) // MICRO_TOKENS
+
+    row_ids, column_ids = iota((width, 1), 0), iota((1, width), 1)
+    row_unit, column_unit = unit(row_ids), unit(column_ids)
+    row_place, column_place = lax.rem(row_ids, MICRO_TOKENS), lax.rem(column_ids, MICRO_TOKENS)
+    column_target = total_of(iota((micros, width), 0) == column_unit, target_column, 0)
+    move[...] = jnp.where(
+        (row_unit.astype(f32) == column_target) & (row_place == column_place), 1.0, 0.0
+    ).astype(bf16)
+    home_micro = jnp.zeros((1, micros), f32)
+    own_bucket = jnp.int32(0)
+    for a in range(home_row.shape[0]):
+        home_micro = home_micro + jnp.where(adapter[...] == a, home_row[a].astype(f32), 0.0)
+        own_bucket = own_bucket + jnp.where(home_row[a] == me, bucket[a], 0)
+    chosen = row_unit.astype(f32) == target_row
+    counted = total_of(chosen, live_count[...].astype(f32), 1)
+    live = row_place.astype(f32) < counted
+    home_here = total_of(chosen, home_micro, 1)
+    self_id = me.astype(f32)
+    mine = jnp.where(live & (home_here == self_id), 1.0, 0.0)
+    own_live = jnp.where(live, 1.0, 0.0)[0:rows, :]
+    micro_home = total_of(iota((width, micros), 1) == row_unit, home_micro, 1)
+    micro_mine = jnp.where(micro_home == self_id, 1.0, 0.0)
+    kept = RANK_LOW * jnp.where(own_bucket == 0, 1, jnp.where(own_bucket == 1, 4, 16))
+    columns = jnp.where(iota((1, rank), 1) < kept, 1.0, 0.0)
+    scale = jnp.where(own_bucket == 0, 4.0, jnp.where(own_bucket == 1, 2.0, 1.0))
+
+    middle_load.wait()
+    backward(MIDDLE, 1)
+    near_load.wait()
+    backward(NEAR, 2)
     x_chip.wait_recv()
     x_last.start()
-
-    middle_load.wait()
-    backward(MIDDLE, 1)
-
-    @pl.when(spot == 0)
-    def _():
-        up_sum[0] = part[MIDDLE]
-        up_middle.start()
-
-    @pl.when(spot == 3)
-    def _():
-        down_sum[0] = part[MIDDLE]
-        down_middle.start()
-
+    dy_chip.start()
     x_core.wait_recv()
     x_last.wait_recv()
 
@@ -225,12 +338,51 @@
     tiles(features, pack)
     pl.when(spot < 3)(up_gather[0].start)
     pl.when(spot > 0)(down_gather[0].start)
-    narrow[:, 0:rank] = (nn(x_all[...], down[...]) * micro_mine[...]).astype(bf16)
-
-    near_load.wait()
-    backward(NEAR, 2)
+    narrow[0] = (nn(x_all[...], down[...]) * micro_mine).astype(bf16)
+    u_steps[0].start()
+    send_peer(0, u_steps)
+    own_load.wait()
+    backward(OWN, 0)
+    send_spread(0, u_steps)
+    forward(spot, 0, first=True)
     dy_chip.wait_recv()
     dy_last.start()
+    dy_core.wait_recv()
+    dy_last.wait_recv()
+    narrow[1] = (nt(dy_all[...], up[...]) * mine).astype(bf16)
+    g_steps[0].start()
+    pass_on(1)
+
+    @pl.when(spot == 0)
+    def _():
+        up_sum[0] = part[MIDDLE]
+        up_middle.start()
+
+    @pl.when(spot == 3)
+    def _():
+        down_sum[0] = part[MIDDLE]
+        down_middle.start()
+
+    send_peer(1, g_steps)
+    send_total(0, u_steps)
+    send_spread(1, g_steps)
+    send_last(u_steps)
+    forward(near_index, 2)
+    again_load.start()
+    wait_all(u_steps)
+    low_source = (narrow_all[0].astype(f32) * columns).astype(bf16)
+    low_wide = nn(move[...], low_source) * mine
+    low = low_wide.astype(bf16)
+
+    def out_part(at):
+        out_delta[:, at] = (scale * nn(low, up[:, at])).astype(bf16)
+
+    tiles(features, out_part)
+    out_core.start()
+    out_core.wait_recv()
+    add(out_sum, block(out_delta, 1), block(out_pair, 1))
+    out_chip.start()
+    pass_on(2)
 
     @pl.when(spot == 1)
     def _():
@@ -244,14 +396,6 @@
         add(down_sum.at[0], part.at[MIDDLE], down_got.at[0])
         down_middle.start()
 
-    dy_core.wait_recv()
-    dy_last.wait_recv()
-    narrow[:, rank : 2 * rank] = (nt(dy_all[...], up[...]) * mine[...]).astype(bf16)
-    pair = remote(narrow.at[pl.ds(2 * rows, 2 * rows), :], narrow_pair, core)
-    pair.start()
-    own_load.wait()
-    backward(OWN, 0)
-
     @pl.when(spot == 0)
     def _():
         up_sum[1] = part[NEAR]
@@ -262,106 +406,45 @@
         down_sum[1] = part[NEAR]
         down_near.start()
 
-    pair.wait_recv()
-    narrow_sum[...] = narrow[rows : 2 * rows, :] + narrow_pair[rows : 2 * rows, :]
-    peer = remote(narrow_sum, narrow_peer, chip)
-    peer.start()
-    forward(spot, 0, first=True)
-
-    peer.wait_recv()
-    narrow_own[...] = narrow[0:rows, :] + narrow_pair[0:rows, :] + narrow_peer[...]
-    spread = [
-        remote(narrow_own, narrow_got.at[k - 1], {"tensor": lax.rem(spot + k, 4)})
-        for k in (1, 2, 3)
-    ]
-    for copy in spread:
-        copy.start()
-
-    @pl.when((spot == 1) | (spot == 2))
-    def _():
-        up_middle.wait_recv()
-        down_middle.wait_recv()
-
-    @pl.when(spot == 1)
-    def _():
-        add(up_sum.at[1], part.at[NEAR], up_got.at[1])
-        add(down_sum.at[1], part.at[FAR], down_got.at[1])
-        up_near.start()
-        down_near.start()
-
-    @pl.when(spot == 2)
-    def _():
-        add(up_sum.at[1], part.at[FAR], up_got.at[1])
-        add(down_sum.at[1], part.at[NEAR], down_got.at[1])
-        up_near.start()
-        down_near.start()
-
-    def pass_on(k):
-        @pl.when(spot >= k)
-        def _():
-            up_gather[k - 1].wait_recv()
-
-        @pl.when(spot <= 3 - k)
-        def _():
-            down_gather[k - 1].wait_recv()
-
-        if k < 3:
-            pl.when((spot >= k) & (spot < 3))(up_gather[k].start)
-            pl.when((spot <= 3 - k) & (spot > 0))(down_gather[k].start)
-
-    pass_on(1)
-    forward(near_index, 2)
-    again_load.start()
-
-    for copy in spread:
-        copy.wait_recv()
-    total = narrow_own[...].astype(f32)
-    for k in range(3):
-        total = total + narrow_got[k].astype(f32)
-    narrow_all[0:rows, :] = total.astype(bf16)
-    all_chip = remote(block(narrow_all, 0), block(narrow_all, 1), chip)
-    all_core = remote(block(narrow_all, 0), block(narrow_all, 2), core)
-    all_last = remote(block(narrow_all, 1), block(narrow_all, 3), core)
-    all_chip.start()
-    all_core.start()
-    all_chip.wait_recv()
-    all_last.start()
-    pass_on(2)
-    all_core.wait_recv()
-    all_last.wait_recv()
-
-    low_source = (narrow_all[:, 0:rank].astype(f32) * columns[...]).astype(bf16)
-    low_wide = nn(move[...], low_source) * mine[...]
-    low = low_wide.astype(bf16)
-    factor = columns[...] * scale[...]
-    grad_low_wide = narrow_all[:, rank : 2 * rank].astype(f32) * factor * mine[...]
+    send_total(1, g_steps)
+    send_last(g_steps)
+    wait_all(g_steps)
+    grad_low_wide = narrow_all[1].astype(f32) * (columns * scale) * mine
     grad_low = grad_low_wide.astype(bf16)
 
-    def deltas(at):
-        out_delta[:, at] = (scale[...] * nn(low, up[:, at])).astype(bf16)
+    def back_part(at):
         back_delta[:, at] = nt(grad_low, down[at, :]).astype(bf16)
 
-    tiles(features, deltas)
-    second = pl.ds(2 * rows, 2 * rows)
-    out_core = remote(out_delta.at[second, :], out_pair, core)
-    back_core = remote(back_delta.at[second, :], back_pair, core)
-    out_core.start()
+    tiles(features, back_part)
     back_core.start()
     forward(middle_index, 1)
-    out_core.wait_recv()
-    add(out_sum, block(out_delta, 1), block(out_pair, 1))
-    out_chip = remote(out_sum, out_peer, chip)
-    out_chip.start()
     back_core.wait_recv()
     add(back_sum, block(back_delta, 1), block(back_pair, 1))
-    back_chip = remote(back_sum, back_peer, chip)
     back_chip.start()
+
+    @pl.when(spot == 1)
+    def _():
+        up_middle.wait_recv()
+        add(up_sum.at[1], part.at[NEAR], up_got.at[1])
+        up_near.start()
+        down_middle.wait_recv()
+        add(down_sum.at[1], part.at[FAR], down_got.at[1])
+        down_near.start()
+
+    @pl.when(spot == 2)
+    def _():
+        down_middle.wait_recv()
+        add(down_sum.at[1], part.at[NEAR], down_got.at[1])
+        down_near.start()
+        up_middle.wait_recv()
+        add(up_sum.at[1], part.at[FAR], up_got.at[1])
+        up_near.start()
 
     low_turned = low_wide.T.astype(bf16)
     grad_turned = nn(grad_low_wide.T.astype(bf16), move[...]).astype(bf16)
 
     def gradients(at):
-        grad_b[:, at] = (scale[...] * nn(low_turned, dy_all[:, at])).astype(bf16)
+        grad_b[:, at] = (scale * nn(low_turned, dy_all[:, at])).astype(bf16)
         grad_a[at, :] = nn(grad_turned, x_all[:, at]).T.astype(bf16)
 
     tiles(features, gradients)
@@ -373,7 +456,7 @@
     def finish_out(at):
         delta = out_delta[0:rows, at].astype(f32) + out_pair[0:rows, at].astype(f32)
         delta = delta + out_peer[:, at].astype(f32)
-        outputs[:, at] = (own_live[...] * (base[:, at] + delta)).astype(bf16)
+        outputs[:, at] = (own_live * (base[:, at] + delta)).astype(bf16)
 
     tiles(features, finish_out)
     base[...] = part[OWN].astype(f32)
@@ -393,13 +476,16 @@
     def finish_back(at):
         delta = back_delta[0:rows, at].astype(f32) + back_pair[0:rows, at].astype(f32)
         delta = delta + back_peer[:, at].astype(f32)
-        input_gradient[:, at] = (own_live[...] * (base[:, at] + delta)).astype(bf16)
+        input_gradient[:, at] = (own_live * (base[:, at] + delta)).astype(bf16)
 
     tiles(features, finish_back)
 
-    for copy in (x_chip, x_core, x_last, dy_chip, dy_core, dy_last, pair, peer, *spread):
+    for copy in (x_chip, x_core, x_last, dy_chip, dy_core, dy_last):
         copy.wait_send()
-    for copy in (all_chip, all_core, all_last, out_core, out_chip, back_core, back_chip):
+    for pair, peer, spread, *rest in (u_steps, g_steps):
+        for copy in (pair, peer, *spread, *rest):
+            copy.wait_send()
+    for copy in (out_core, out_chip, back_core, back_chip):
         copy.wait_send()
     pl.when(spot == 0)(up_far.wait_send)
     pl.when(spot == 3)(down_far.wait_send)
@@ -421,6 +507,7 @@
         return pltpu.VMEM(shape, bf16)
 
     vmem = pl.BlockSpec(memory_space=pltpu.VMEM)
+    smem = pl.BlockSpec(memory_space=pltpu.SMEM)
     all_rows = 4 * rows
     return pl.pallas_call(
         layer_kernel,
@@ -430,7 +517,7 @@
             jax.ShapeDtypeStruct((features, rank), bf16),
             jax.ShapeDtypeStruct((rank, features), bf16),
         ),
-        in_specs=[vmem, vmem, pl.BlockSpec(memory_space=pl.ANY)] + [vmem] * (2 + len(rest)),
+        in_specs=[vmem, vmem, pl.BlockSpec(memory_space=pl.ANY)] + [vmem] * 5 + [smem] * 2,
         out_specs=(vmem,) * 4,
         scratch_shapes=[
             held(all_rows, features),
@@ -442,13 +529,14 @@
             held(2, rows, features),
             held(2, rows, features),
             held(3, features, features),
-            held(all_rows, 2 * rank),
-            held(2 * rows, 2 * rank),
-            held(rows, 2 * rank),
-            held(rows, 2 * rank),
-            held(rows, 2 * rank),
-            held(3, rows, 2 * rank),
-            held(all_rows, 2 * rank),
+            held(all_rows, all_rows),
+            held(2, all_rows, rank),
+            held(2, 2 * rows, rank),
+            held(2, rows, rank),
+            held(2, rows, rank),
+            held(2, rows, rank),
+            held(2, 3, rows, rank),
+            held(2, all_rows, rank),
             held(all_rows, features),
             held(2 * rows, features),
             held(rows, features),
@@ -459,14 +547,47 @@
             held(rows, features),
             pltpu.VMEM((rows, features), jnp.float32),
             pltpu.SemaphoreType.DMA((5,)),
-            pltpu.SemaphoreType.DMA((40,)),
-            pltpu.SemaphoreType.DMA((40,)),
+            pltpu.SemaphoreType.DMA((48,)),
+            pltpu.SemaphoreType.DMA((48,)),
         ],
         compiler_params=pltpu.CompilerParams(
             collective_id=0, has_side_effects=True, vmem_limit_bytes=60 * 1024 * 1024
         ),
         name="layer",
     )(tokens, cotangent, weight, down, up, *rest)
+
+
+def hand_on_kernel(count, *refs):
+    sources, results = refs[:count], refs[count : 2 * count]
+    held, sems = refs[2 * count : 3 * count], refs[3 * count]
+    loads = [
+        pltpu.make_async_copy(sources[i], held[i], sems.at[2 * i]) for i in range(count)
+    ]
+    stores = [
+        pltpu.make_async_copy(held[i], results[i], sems.at[2 * i + 1]) for i in range(count)
+    ]
+    for copy in loads:
+        copy.start()
+    for load, store in zip(loads, stores):
+        load.wait()
+        store.start()
+    for copy in stores:
+        copy.wait()
+
+
+def handed_on(*arrays):
+    anywhere = pl.BlockSpec(memory_space=pltpu.HBM)
+    count = len(arrays)
+    return pl.pallas_call(
+        functools.partial(hand_on_kernel, count),
+        out_shape=tuple(jax.ShapeDtypeStruct(a.shape, a.dtype) for a in arrays),
+        in_specs=[anywhere] * count,
+        out_specs=(anywhere,) * count,
+        scratch_shapes=[pltpu.VMEM(a.shape, a.dtype) for a in arrays]
+        + [pltpu.SemaphoreType.DMA((2 * count,))],
+        compiler_params=pltpu.CompilerParams(vmem_limit_bytes=32 * 1024 * 1024),
+        name="hand_on",
+    )(*arrays)
 
 
 def local(
@@ -488,6 +609,15 @@
     own_rows = cotangent.shape[0]
     f32, bf16 = jnp.float32, jnp.bfloat16
     down, up = adapter_down_factor[0], adapter_up_factor[0]
+    if n == 4 and n_tensor == 4 and tokens.shape == cotangent.shape:
+        outputs, input_gradient, grad_a, grad_b = handed_on(
+            *layer(
+                tokens, cotangent, weight, down, up, micro_destination_group,
+                micro_adapter.reshape(1, -1), micro_token_count.reshape(1, -1),
+                adapter_rank_bucket, adapter_home_row,
+            )
+        )
+        return outputs, input_gradient, grad_a[None], grad_b[None]
 
     micro_target, micro_home, slot_ids, home, counted = packing(
         micro_destination_group, micro_adapter, micro_token_count, adapter_home_row, n, me
@@ -506,13 +636,6 @@
     rank = RANK_LOW * jnp.where(bucket == 0, 1, jnp.where(bucket == 1, 4, 16))
     scale = jnp.sqrt(LARGEST_RANK / rank.astype(f32))
     columns = (jnp.arange(LARGEST_RANK, dtype=jnp.int32) < rank).astype(f32)[None, :]
-
-    if n == 4 and n_tensor == 4 and tokens.shape == cotangent.shape:
-        outputs, input_gradient, grad_a, grad_b = layer(
-            tokens, cotangent, weight, down, up, move, micro_mine, mine, own_live, columns,
-            scale.reshape(1, 1),
-        )
-        return outputs, input_gradient, grad_a[None], grad_b[None]
 
     x_all = gather_blocks(tokens, n)
     dy_all = gather_blocks(cotangent, n)

time: 134 us -> 98.3 us (0.73)
  the two profiles are of different devices: /device:TPU:10 before, /device:TPU:0 now
where the time goes in v2:
time: 98.3 us; the launch traced here: 98 us
  Pallas kernels  91.5 us (93%)
  local copies, waits for them, and re-layouts  5.86 us (6%)
    pallas_call x1, Pallas kernels, layer(): pl.pallas_call(layer_kernel, out_shape=(jax.ShapeDtypeStruct((rows, featu...  89.6 us
    unnamed x9, local copies, waits for them, and re-layouts  5.86 us

profile of v2, /device:TPU:0, one launch (start us, length us, event | category | flops | bytes accessed | tf_op | source)
XLA Modules:
  0.0 98.0 jit_solution(10020899746142971855)
XLA Ops:
  0.6 1.3 %copy.14.destination = s32[32,1]{1,0:T(8,128)} copy(s32[32,1]{0,1:T(1,128)} %param.15) | data formatting | bytes 256 | tf_op args[5]
  2.0 89.6 %layer.1 = (bf16[128,2048]{1,0:T(8,128)(2,1)}, bf16[128,2048]{1,0:T(8,128)(2,1)}, bf16[2048,256]{1,0:T(8,128)(2,1)}, bf16[256,2048]{1,0:T(8,128)(2,1)}) custom-call(bf16[128,2048]{1,0:T(8,128)(2,1)} %tokens.1, bf16[128,2048]{1,0:T(8,128)(2,1)} %cotangent.1, bf16[8192,2048]{1,0:T(8,128)(2,1)} %weight.1, bf16[2048,256]{1,0:T(8,128)(2,1)} %bitcast.6, ...), custom_call_target="tpu_custom_call" | custom-call | tf_op jit(solution)/shard_map/layer/pallas_call | solution.py:512
  91.5 0.0 copy-start
  91.6 1.2 %copy-done = bf16[2048,256]{1,0:T(8,128)(2,1)S(1)} copy-done((bf16[2048,256]{1,0:T(8,128)(2,1)S(1)}, bf16[2048,256]{1,0:T(8,128)(2,1)}, u32[]{:S(2)}) %copy-start) | copy-done | bytes 1048600
  92.8 0.0 copy-start.1
  92.8 1.2 %copy-done.1 = bf16[256,2048]{1,0:T(8,128)(2,1)S(1)} copy-done((bf16[256,2048]{1,0:T(8,128)(2,1)S(1)}, bf16[256,2048]{1,0:T(8,128)(2,1)}, u32[]{:S(2)}) %copy-start.1) | copy-done | bytes 1048600
  94.0 0.0 copy-start.2
  94.0 1.0 %copy-done.2 = bf16[128,2048]{1,0:T(8,128)(2,1)S(1)} copy-done((bf16[128,2048]{1,0:T(8,128)(2,1)S(1)}, bf16[128,2048]{1,0:T(8,128)(2,1)}, u32[]{:S(2)}) %copy-start.2) | copy-done | bytes 524312
  95.0 0.0 copy-start.3
  95.0 1.0 %copy-done.3 = bf16[128,2048]{1,0:T(8,128)(2,1)S(1)} copy-done((bf16[128,2048]{1,0:T(8,128)(2,1)S(1)}, bf16[128,2048]{1,0:T(8,128)(2,1)}, u32[]{:S(2)}) %copy-start.3) | copy-done | bytes 524312
  96.1 1.9 %hand_on.1 = (bf16[128,2048]{1,0:T(8,128)(2,1)}, bf16[128,2048]{1,0:T(8,128)(2,1)}, bf16[2048,256]{1,0:T(8,128)(2,1)}, bf16[256,2048]{1,0:T(8,128)(2,1)}) custom-call(bf16[128,2048]{1,0:T(8,128)(2,1)S(1)} %copy-done.2, bf16[128,2048]{1,0:T(8,128)(2,1)S(1)} %copy-done.3, bf16[2048,256]{1,0:T(8,128)(2,1)S(1)} %copy-done, bf16[256,2048]{1,0:T(8,128)(2,1)S(1)} %copy-done.1), custom_call_target="tpu_custom_call" | custom-call | tf_op jit(solution)/shard_map/hand_on/pallas_call | solution.py:581
Async XLA Ops:
  91.5 1.2 %copy-start = (bf16[2048,256]{1,0:T(8,128)(2,1)S(1)}, bf16[2048,256]{1,0:T(8,128)(2,1)}, u32[]{:S(2)}) copy-start(bf16[2048,256]{1,0:T(8,128)(2,1)} %get-tuple-element.14.refs_2_) | copy-start | bytes 3145732
  92.8 1.2 %copy-start.1 = (bf16[256,2048]{1,0:T(8,128)(2,1)S(1)}, bf16[256,2048]{1,0:T(8,128)(2,1)}, u32[]{:S(2)}) copy-start(bf16[256,2048]{1,0:T(8,128)(2,1)} %get-tuple-element.15.refs_3_) | copy-start | bytes 3145732
  94.0 1.0 %copy-start.2 = (bf16[128,2048]{1,0:T(8,128)(2,1)S(1)}, bf16[128,2048]{1,0:T(8,128)(2,1)}, u32[]{:S(2)}) copy-start(bf16[128,2048]{1,0:T(8,128)(2,1)} %get-tuple-element.12.refs_0_) | copy-start | bytes 1572868
  95.0 1.0 %copy-start.3 = (bf16[128,2048]{1,0:T(8,128)(2,1)S(1)}, bf16[128,2048]{1,0:T(8,128)(2,1)}, u32[]{:S(2)}) copy-start(bf16[128,2048]{1,0:T(8,128)(2,1)} %get-tuple-element.13.refs_1_) | copy-start | bytes 1572868

commit v3 on v2

--- a/solution.py
+++ b/solution.py
@@ -324,8 +324,6 @@
 
     middle_load.wait()
     backward(MIDDLE, 1)
-    near_load.wait()
-    backward(NEAR, 2)
     x_chip.wait_recv()
     x_last.start()
     dy_chip.start()
@@ -340,6 +338,8 @@
     pl.when(spot > 0)(down_gather[0].start)
     narrow[0] = (nn(x_all[...], down[...]) * micro_mine).astype(bf16)
     u_steps[0].start()
+    near_load.wait()
+    backward(NEAR, 2)
     send_peer(0, u_steps)
     own_load.wait()
     backward(OWN, 0)

time: 98.3 us -> 98 us (level)
  no operation moved by 1% of the time
where the time goes in v3:
time: 98 us; the launch traced here: 97.7 us
  Pallas kernels  91.2 us (93%)
  local copies, waits for them, and re-layouts  5.86 us (6%)
    pallas_call x1, Pallas kernels, layer(): pl.pallas_call(layer_kernel, out_shape=(jax.ShapeDtypeStruct((rows, featu...  89.3 us
    unnamed x9, local copies, waits for them, and re-layouts  5.86 us

profile of v3, /device:TPU:0, one launch (start us, length us, event | category | flops | bytes accessed | tf_op | source)
XLA Modules:
  0.0 97.7 jit_solution(6457046607912260376)
XLA Ops:
  0.6 1.3 %copy.14.destination = s32[32,1]{1,0:T(8,128)} copy(s32[32,1]{0,1:T(1,128)} %param.15) | data formatting | bytes 256 | tf_op args[5]
  2.0 89.3 %layer.1 = (bf16[128,2048]{1,0:T(8,128)(2,1)}, bf16[128,2048]{1,0:T(8,128)(2,1)}, bf16[2048,256]{1,0:T(8,128)(2,1)}, bf16[256,2048]{1,0:T(8,128)(2,1)}) custom-call(bf16[128,2048]{1,0:T(8,128)(2,1)} %tokens.1, bf16[128,2048]{1,0:T(8,128)(2,1)} %cotangent.1, bf16[8192,2048]{1,0:T(8,128)(2,1)} %weight.1, bf16[2048,256]{1,0:T(8,128)(2,1)} %bitcast.6, ...), custom_call_target="tpu_custom_call" | custom-call | tf_op jit(solution)/shard_map/layer/pallas_call | solution.py:512
  91.3 0.0 copy-start
  91.3 1.2 %copy-done = bf16[2048,256]{1,0:T(8,128)(2,1)S(1)} copy-done((bf16[2048,256]{1,0:T(8,128)(2,1)S(1)}, bf16[2048,256]{1,0:T(8,128)(2,1)}, u32[]{:S(2)}) %copy-start) | copy-done | bytes 1048600
  92.5 0.0 copy-start.1
  92.5 1.2 %copy-done.1 = bf16[256,2048]{1,0:T(8,128)(2,1)S(1)} copy-done((bf16[256,2048]{1,0:T(8,128)(2,1)S(1)}, bf16[256,2048]{1,0:T(8,128)(2,1)}, u32[]{:S(2)}) %copy-start.1) | copy-done | bytes 1048600
  93.7 0.0 copy-start.2
  93.7 1.0 %copy-done.2 = bf16[128,2048]{1,0:T(8,128)(2,1)S(1)} copy-done((bf16[128,2048]{1,0:T(8,128)(2,1)S(1)}, bf16[128,2048]{1,0:T(8,128)(2,1)}, u32[]{:S(2)}) %copy-start.2) | copy-done | bytes 524312
  94.7 0.0 copy-start.3
  94.8 1.0 %copy-done.3 = bf16[128,2048]{1,0:T(8,128)(2,1)S(1)} copy-done((bf16[128,2048]{1,0:T(8,128)(2,1)S(1)}, bf16[128,2048]{1,0:T(8,128)(2,1)}, u32[]{:S(2)}) %copy-start.3) | copy-done | bytes 524312
  95.8 1.9 %hand_on.1 = (bf16[128,2048]{1,0:T(8,128)(2,1)}, bf16[128,2048]{1,0:T(8,128)(2,1)}, bf16[2048,256]{1,0:T(8,128)(2,1)}, bf16[256,2048]{1,0:T(8,128)(2,1)}) custom-call(bf16[128,2048]{1,0:T(8,128)(2,1)S(1)} %copy-done.2, bf16[128,2048]{1,0:T(8,128)(2,1)S(1)} %copy-done.3, bf16[2048,256]{1,0:T(8,128)(2,1)S(1)} %copy-done, bf16[256,2048]{1,0:T(8,128)(2,1)S(1)} %copy-done.1), custom_call_target="tpu_custom_call" | custom-call | tf_op jit(solution)/shard_map/hand_on/pallas_call | solution.py:581
Async XLA Ops:
  91.3 1.2 %copy-start = (bf16[2048,256]{1,0:T(8,128)(2,1)S(1)}, bf16[2048,256]{1,0:T(8,128)(2,1)}, u32[]{:S(2)}) copy-start(bf16[2048,256]{1,0:T(8,128)(2,1)} %get-tuple-element.14.refs_2_) | copy-start | bytes 3145732
  92.5 1.2 %copy-start.1 = (bf16[256,2048]{1,0:T(8,128)(2,1)S(1)}, bf16[256,2048]{1,0:T(8,128)(2,1)}, u32[]{:S(2)}) copy-start(bf16[256,2048]{1,0:T(8,128)(2,1)} %get-tuple-element.15.refs_3_) | copy-start | bytes 3145732
  93.7 1.0 %copy-start.2 = (bf16[128,2048]{1,0:T(8,128)(2,1)S(1)}, bf16[128,2048]{1,0:T(8,128)(2,1)}, u32[]{:S(2)}) copy-start(bf16[128,2048]{1,0:T(8,128)(2,1)} %get-tuple-element.12.refs_0_) | copy-start | bytes 1572868
  94.7 1.0 %copy-start.3 = (bf16[128,2048]{1,0:T(8,128)(2,1)S(1)}, bf16[128,2048]{1,0:T(8,128)(2,1)}, u32[]{:S(2)}) copy-start(bf16[128,2048]{1,0:T(8,128)(2,1)} %get-tuple-element.13.refs_1_) | copy-start | bytes 1572868
